TPU v7x, 128 devices: a whole 4x4x4 slice. The times are simulated.
128 devices in a mesh: gx: 8 (over x, core), gy: 16 (over z, y).
Axes of the slice: x: 4, y: 4, z: 4, core: 2. Of those that a mesh axis runs over, the one named last changes fastest.
Arguments:
- features: bfloat16 [128, 256, 64, 128], P('gx', 'gy'), may hold values from -6 to 6
- occupancy: int32 [128, 256, 64], P('gx', 'gy'), may hold values 0 or 1
- weight: bfloat16 [27, 128, 256], replicated, may hold values from -0.109375 to 0.109375
- owner: int32 [8, 16, 32], P('gx', 'gy'), may hold values from 0 to 15, as said below
- cotangent: bfloat16 [8, 16, 48, 16384], P('gx', 'gy'), may hold values from -6 to 6
Outputs:
- owned_output: bfloat16 [8, 16, 48, 16384], P('gx', 'gy')
- grad_input: bfloat16 [128, 256, 64, 128], P('gx', 'gy')
- grad_weight: float32 [27, 128, 256], replicated
Inputs may be any that keep to these rules, and one draw needn't show every extreme that they name: Each device sends at most 3 of its 32 output bricks to any one owner; one owner receives exactly 3 bricks from every device of its gx index.
All inputs are finite; a program needn't handle non-finite values. No bound on the sum of `occupancy` on one device may be relied on, other than what follows from the above.
Results may differ from a plain program's by a relative error of at most 0.0035.
Values may be sent and summed in bfloat16 or wider, within the bound.
A program may use at most 192 MiB of HBM per device.

v0:
```python
import jax
import jax.numpy as jnp
from jax import lax
from jax.experimental import pallas as pl
from jax.experimental.pallas import tpu as pltpu
from jax.sharding import PartitionSpec as P

BF = jnp.bfloat16
F32 = jnp.float32
MESH = pl.DeviceIdType.MESH
TAPS = 27
TILES = 54


def iota2(shape, dim):
    return lax.broadcasted_iota(jnp.int32, shape, dim)


def as_bf(cond):
    return jnp.where(cond, 1.0, 0.0).astype(F32).astype(BF)


def dot(a, b):
    return jnp.dot(a, b, preferred_element_type=F32)


def dot_nt(a, b):
    return lax.dot_general(a, b, (((1,), (1,)), ((), ())), preferred_element_type=F32)


def row_coords(rows):
    return rows // 128, (rows // 16) % 8, (rows // 4) % 4, rows % 4


def kernel(
    n_gx, n_gy, cap, per,
    slot_ref, inv_ref, occ_ref, feat, weight, cot,
    owned_out, gin_out, gw_out,
    fp, pt, mk, act, bk, cv, csend, ret, outg, arr, wv, ub, yhu, ysu, uu, upt,
    xs, ys, gi, dwf, s1s, s1r, s2s, s2r, s3s, s3r, ag, gws, pk, pc, po, qs, pysel,
    sem_feat, sem_in, sem_loc, sem_out, sem_gi, sem_gw,
    a1_s, a1_r, a2_s, a2_r, h_s, h_r, u_s, u_r,
    r1_s, r1_r, r2_s, r2_r, r3_s, r3_r, g4_s, g4_r, g5_s, g5_r, g6_s, g6_r,
):
    n_x = n_gx // 2
    i = lax.axis_index("gx")
    j = lax.axis_index("gy")
    xq = i // 2
    core = lax.rem(i, 2)
    sib = 2 * xq + 1 - core
    nxt_i, prv_i = lax.rem(i + 1, n_gx), lax.rem(i + n_gx - 1, n_gx)
    nxt_j, prv_j = lax.rem(j + 1, n_gy), lax.rem(j + n_gy - 1, n_gy)

    cot_copy = pltpu.make_async_copy(cot.at[0, 0], cv, sem_in.at[0])
    cot_copy.start()

    def feat_copy(x):
        return pltpu.make_async_copy(feat.at[x], fp.at[x + 1, pl.ds(1, 16)], sem_feat.at[x])

    for x in range(15, -1, -1):
        feat_copy(x).start()
    w_copy = pltpu.make_async_copy(weight, wv, sem_in.at[1])
    w_copy.start()

    barrier = pltpu.get_barrier_semaphore()
    peers = [(i, lax.rem(j + d, n_gy)) for d in range(1, n_gy)]
    peers += [(lax.rem(i + d, n_gx), j) for d in range(2, n_gx - 1, 2)]
    peers += [(nxt_i, j), (prv_i, j), (nxt_i, nxt_j), (prv_i, prv_j)]
    for peer in peers:
        pl.semaphore_signal(barrier, inc=1, device_id=peer, device_id_type=MESH)

    r, c = iota2((128, 256), 0), iota2((128, 256), 1)
    _, bz, vy, vz = row_coords(r)
    oz = 4 * bz + vz
    for kz in range(3):
        pk[kz] = as_bf((vy == c // 64) & (2 * oz + kz - 1 == c % 64))
    pk[3] = as_bf((vy == c // 64) & (oz == (c % 64) // 2))
    r, c = iota2((256, 256), 0), iota2((256, 256), 1)
    pc[0] = as_bf((r // 16 == c % 16) & (r % 16 == c // 16))
    pc[1] = as_bf(r == c)
    _, cbz, cvy, cvz = row_coords(c % 128)
    po[...] = as_bf((cvy == r // 64) & (8 * cbz + 2 * cvz + c // 128 == r % 64))
    rby, rbz, rvy, rvz = row_coords(r)
    cby, cbz, cvy, cvz = row_coords(c)
    roz, coz = 4 * rbz + rvz, 4 * cbz + cvz
    roy, coy = 4 * rby + rvy, 4 * cby + cvy
    qs[0] = as_bf((roy == coy) & (roz + 1 == coz))
    qs[1] = as_bf((roy + 1 == coy) & (roz == coz))
    qs[2] = as_bf((roy + 1 == coy) & (roz + 1 == coz))
    r, c = iota2((256, 128), 0), iota2((256, 128), 1)
    rby, rbz, rvy, rvz = row_coords(r)
    top = (4 * rby + rvy == 7) & (c < 32)
    qs[3, :, 0:128] = as_bf(top & (4 * rbz + rvz == c))
    qs[3, :, 128:256] = as_bf(top & (4 * rbz + rvz + 1 == c))
    r, c = iota2((128, 128), 0), iota2((128, 128), 1)
    _, cbz, cvy, cvz = row_coords(c)
    pysel[...] = as_bf((r < 32) & (cvy == 0) & (4 * cbz + cvz == r))

    pl.semaphore_wait(barrier, len(peers))

    cot_copy.wait()

    def cot_step(n, carry):
        t, vg = n // 4, n % 4
        rhs = jnp.concatenate(
            [
                cv[pl.ds(pl.multiple_of(16 * t, 16), 16), pl.ds(pl.multiple_of(4096 * vg + 256 * v, 256), 256)]
                for v in range(16)
            ],
            0,
        )
        res = dot(pc[0], rhs).astype(BF).reshape(16, 16, 256)
        csend[pl.ds(16 * t, 16), pl.ds(pl.multiple_of(16 * vg, 16), 16), :] = res
        return carry

    lax.fori_loop(0, 12, cot_step, 0)

    def a2a(d, src, dst, s_sem, r_sem):
        to = lax.rem(j + d, n_gy)
        return pltpu.make_async_remote_copy(
            src_ref=src.at[pl.ds(to * cap, cap)],
            dst_ref=dst.at[pl.ds(j * cap, cap)],
            send_sem=s_sem.at[d],
            recv_sem=r_sem.at[d],
            device_id=(i, to),
            device_id_type=MESH,
        )

    def a2a_arrival(d, src, dst, s_sem, r_sem):
        frm = lax.rem(j - d + n_gy, n_gy)
        return pltpu.make_async_remote_copy(
            src_ref=src.at[pl.ds(frm * cap, cap)],
            dst_ref=dst.at[pl.ds(frm * cap, cap)],
            send_sem=s_sem.at[d],
            recv_sem=r_sem.at[d],
            device_id=(i, frm),
            device_id_type=MESH,
        )

    for d in range(1, n_gy):
        a2a(d, csend, ret, a1_s, a1_r).start()
    own1 = pltpu.make_async_copy(
        csend.at[pl.ds(j * cap, cap)], ret.at[pl.ds(j * cap, cap)], sem_loc.at[0]
    )
    own1.start()

    def occ_row(x, y):
        return occ_ref[x, pl.ds(y, 1), :].astype(F32)

    def lanes_of(rows):
        return jnp.concatenate(rows, 1)

    def wide(row):
        return jnp.broadcast_to(row, (16, 256)).astype(BF)

    def masked_rows(mat, row):
        rows = mat.shape[0]
        m = wide(row)
        return (mat.reshape(rows // 16, 16, 256) * m[None]).reshape(rows, 256)

    feat_copy(15).wait()
    for by in range(2):
        for py in range(2):
            row = lanes_of([occ_row(15, 8 * by + 2 * v + py) for v in range(4)])
            rhs = jnp.concatenate([fp[16, 1 + 8 * by + 2 * v + py] for v in range(4)], 0)
            res = dot(masked_rows(pc[1], row), rhs).astype(BF)
            for v in range(4):
                xs[8 * by + 2 * v + py] = res[64 * v : 64 * v + 64]

    def remote(src, dst, s_sem, r_sem, to):
        return pltpu.make_async_remote_copy(
            src_ref=src, dst_ref=dst, send_sem=s_sem, recv_sem=r_sem,
            device_id=to, device_id_type=MESH,
        )

    halo_x = remote(xs, fp.at[0, pl.ds(1, 16)], h_s.at[0], h_r.at[0], (nxt_i, j))
    halo_x.start()
    for x in range(14, -1, -1):
        feat_copy(x).wait()

    def mask_y(x, carry):
        row = lanes_of([occ_row(x, 9 + 2 * v) for v in range(4)])
        rhs = jnp.concatenate([fp[x + 1, 10 + 2 * v] for v in range(4)], 0)
        ys[x] = dot(masked_rows(pc[1, 192:256, :], row), rhs).astype(BF)
        return carry

    lax.fori_loop(0, 16, mask_y, 0)
    halo_y = remote(ys, fp.at[pl.ds(1, 16), 0], h_s.at[1], h_r.at[1], (i, nxt_j))
    halo_y.start()
    halo_c = remote(ys.at[15], fp.at[0, 0], h_s.at[2], h_r.at[2], (nxt_i, nxt_j))
    halo_c.start()

    ones = jnp.ones((256, 128), F32).astype(BF)

    def prep(xp, by, ky, row, own):
        rhs = jnp.concatenate([fp[xp, 8 * by + 2 * v + ky] for v in range(4)], 0)
        with_mask = own and ky > 0
        if with_mask:
            rhs = jnp.concatenate([rhs, ones], 1)
        for kz in range(3):
            res = dot(masked_rows(pk[kz], row), rhs if kz > 0 or not with_mask else rhs[:, :128])
            col = (3 * ky + kz) * 128
            pt[xp, by * 128 : by * 128 + 128, col : col + 128] = res[:, :128].astype(BF)
            if with_mask and kz > 0:
                mk[xp - 1, 2 * (ky - 1) + kz - 1, by * 128 : by * 128 + 128, :] = res[:, 128:].astype(BF)

    def prep_own(x, carry):
        for by, ky in ((0, 1), (0, 2), (1, 0), (1, 1), (1, 2)):
            row = lanes_of([occ_row(x, 8 * by + 2 * v + ky - 1) for v in range(4)])
            prep(x + 1, by, ky, row, True)
        return carry

    lax.fori_loop(0, 16, prep_own, 0)

    def count_active(ox, carry):
        for by in range(2):
            total = jnp.zeros((1, 256), F32)
            for px in range(2):
                for py in range(2):
                    total = total + lanes_of([occ_row(2 * ox + px, 8 * by + 2 * v + py) for v in range(4)])
            count = dot(masked_rows(pk[3], total), ones)
            act[ox, by * 128 : by * 128 + 128, :] = jnp.where(count > 0.5, 1.0, 0.0).astype(BF)
        return carry

    lax.fori_loop(0, 8, count_active, 0)

    ok_x = jnp.where(i > 0, 1.0, 0.0).astype(F32)
    ok_y = jnp.where(j > 0, 1.0, 0.0).astype(F32)
    halo_x.wait()
    halo_y.wait()
    halo_c.wait()

    def prep_halo_y(x, carry):
        row = lanes_of([jnp.full((1, 64), ok_y, F32)] + [occ_row(x, 2 * v + 1) for v in range(3)])
        prep(x + 1, 0, 0, row, False)
        return carry

    lax.fori_loop(0, 16, prep_halo_y, 0)
    row_x = jnp.full((1, 256), ok_x, F32)
    corner = jnp.where(iota2((1, 256), 1) < 64, ok_x * ok_y, ok_x)
    for by in range(2):
        for ky in range(3):
            prep(0, by, ky, corner if (by == 0 and ky == 0) else row_x, False)

    w_copy.wait()

    def forward(ox, carry):
        lhs = jnp.concatenate([pt[2 * ox], pt[2 * ox + 1], pt[2 * ox + 2]], 1)
        acc = dot(lhs, wv[...])
        a = act[ox]
        a = jnp.concatenate([a, a], 1).astype(F32)
        bk[pl.ds(ox * 16, 16)] = (acc * a).astype(BF).reshape(16, 16, 256)
        return carry

    lax.fori_loop(0, 8, forward, 0)

    def pack(s, carry):
        base = inv_ref[s]
        keep = jnp.where(base >= 0, 1.0, 0.0).astype(F32)
        at = jnp.maximum(base, 0)
        flag = jnp.full((16, 256), keep, F32).astype(BF)
        for vx in range(4):
            outg[s, vx * 16 : vx * 16 + 16, :] = bk[at + 16 * vx] * flag
        return carry

    lax.fori_loop(0, n_gy * cap, pack, 0)

    own1.wait()
    for d in range(1, n_gy):
        a2a_arrival(d, csend, ret, a1_s, a1_r).wait_recv()
    for d in range(1, n_gy):
        a2a(d, outg, arr, a2_s, a2_r).start()
    own2 = pltpu.make_async_copy(
        outg.at[pl.ds(j * cap, cap)], arr.at[pl.ds(j * cap, cap)], sem_loc.at[1]
    )
    own2.start()

    def place(b, carry):
        s = slot_ref[b]
        bx, rest = b // 16, b % 16
        for vx in range(4):
            off = pl.multiple_of(rest * 16, 16)
            a = act[bx * 4 + vx, pl.ds(off, 16), :]
            a = jnp.concatenate([a, a], 1)
            ub[bx * 4 + vx, pl.ds(off, 16), :] = ret[s, vx * 16 : vx * 16 + 16, :] * a
        return carry

    lax.fori_loop(0, 32, place, 0)

    for ox in range(8):
        ysu[ox] = dot(pysel[...], ub[ox, 0:128, :])[0:32].astype(BF)
    up_x = remote(ub.at[0], ub.at[8], u_s.at[0], u_r.at[0], (prv_i, j))
    up_y = remote(ysu, yhu.at[pl.ds(0, 8)], u_s.at[1], u_r.at[1], (i, prv_j))
    up_c = remote(ysu.at[0], yhu.at[8], u_s.at[2], u_r.at[2], (prv_i, prv_j))
    up_x.start()
    up_y.start()
    up_c.start()

    for ox in range(8):
        upt[:, ox * 256 : ox * 256 + 256] = dot_nt(pc[1], ub[ox]).astype(BF)

    mine = pl.multiple_of(core * 128, 128)
    other = pl.multiple_of(128 - core * 128, 128)

    def stage1(kx):
        cols = pl.ds(kx * 1152, 1152)
        return remote(s1s.at[:, cols], s1r.at[:, cols], r1_s.at[kx], r1_r.at[kx], (sib, j))

    for kx in range(3):
        for n in range(5):
            width = 256 if n < 4 else 128
            rhs = jnp.concatenate(
                [pt[2 * ox + kx, :, n * 256 : n * 256 + width] for ox in range(8)], 0
            )
            col = kx * 1152 + n * 256
            dwf[:, col : col + width] = dot(upt[...], rhs)
        s1s[:, kx * 1152 : kx * 1152 + 1152] = dwf[pl.ds(other, 128), kx * 1152 : kx * 1152 + 1152].astype(BF)
        stage1(kx).start()

    up_x.wait()
    up_y.wait()
    up_c.wait()
    okn_x = jnp.where(i < n_gx - 1, 1.0, 0.0).astype(F32)
    okn_y = jnp.where(j < n_gy - 1, 1.0, 0.0).astype(F32)

    def shifts(ox, carry):
        last = jnp.where(ox == 8, okn_x, 1.0).astype(F32)
        base = (ub[ox].astype(F32) * last).astype(BF)
        halo = (yhu[ox].astype(F32) * (last * okn_y)).astype(BF)
        halo = jnp.concatenate([halo, jnp.zeros((96, 256), BF)], 0)
        uu[0, ox, :, 0:256] = base
        uu[0, ox, :, 256:512] = dot(qs[0], base).astype(BF)
        uu[1, ox, :, 0:256] = (dot(qs[1], base) + dot(qs[3, :, 0:128], halo)).astype(BF)
        uu[1, ox, :, 256:512] = (dot(qs[2], base) + dot(qs[3, :, 128:256], halo)).astype(BF)
        return carry

    lax.fori_loop(0, 9, shifts, 0)

    lists = (((1, 0),), ((2, 0), (0, 1)))

    def gin_copy(x):
        return pltpu.make_async_copy(gi.at[x], gin_out.at[x], sem_gi.at[x])

    def grad_in(ox, carry):
        for px in range(2):
            for py in range(2):
                both, odd = None, None
                for a, sx in lists[px]:
                    for b, sy in lists[py]:
                        k = 9 * a + 3 * b
                        one = dot_nt(uu[sy, ox + sx, :, 0:256], wv[(k + 1) * 128 : (k + 3) * 128, :])
                        two = dot_nt(uu[sy, ox + sx, :, 256:512], wv[k * 128 : (k + 1) * 128, :])
                        both = one if both is None else both + one
                        odd = two if odd is None else odd + two
                m0 = mk[2 * ox + px, 2 * py].astype(F32)
                m1 = mk[2 * ox + px, 2 * py + 1].astype(F32)
                g0 = (both[:, :128] * m0).astype(BF)
                g1 = ((both[:, 128:] + odd) * m1).astype(BF)
                rhs = jnp.concatenate(
                    [
                        jnp.concatenate([g0[:128], g1[:128]], 0),
                        jnp.concatenate([g0[128:], g1[128:]], 0),
                    ],
                    1,
                )
                res = dot(po[...], rhs).astype(BF)
                for by in range(2):
                    for v in range(4):
                        gi[2 * ox + px, 8 * by + 2 * v + py] = res[64 * v : 64 * v + 64, 128 * by : 128 * by + 128]
            gin_copy(2 * ox + px).start()
        return carry

    lax.fori_loop(0, 2, grad_in, 0)

    def stage2(d):
        to = lax.rem(xq + d, n_x)
        return remote(s2s.at[to], s2r.at[xq], r2_s.at[d], r2_r.at[d], (2 * to + core, j))

    def stage2_arrival(d):
        frm = lax.rem(xq - d + n_x, n_x)
        return remote(s2s.at[frm], s2r.at[frm], r2_s.at[d], r2_r.at[d], (2 * frm + core, j))

    for kx in range(3):
        stage1(kx).wait()

    def sum1(q, carry):
        at = pl.multiple_of(mine + q * s2s.shape[1], 16)
        rows = s2s.shape[1]
        mid = dwf[pl.ds(at, rows), :] + s1r[pl.ds(pl.multiple_of(q * rows, 16), rows), :].astype(F32)
        dwf[pl.ds(at, rows), :] = mid
        s2s[q] = mid.astype(BF)
        return carry

    lax.fori_loop(0, n_x, sum1, 0)
    for d in range(1, n_x):
        stage2(d).start()

    lax.fori_loop(2, 6, grad_in, 0)

    for d in range(1, n_x):
        stage2_arrival(d).wait_recv()
    rows2 = s2s.shape[1]
    for half in range(rows2 // 16):
        at = pl.multiple_of(mine + xq * rows2 + half * 16, 16)
        total = dwf[pl.ds(at, 16), :]
        for d in range(1, n_x):
            frm = lax.rem(xq + d, n_x)
            total = total + s2r[frm, half * 16 : half * 16 + 16, :].astype(F32)
        total = total.astype(BF)
        for tap in range(TAPS):
            s3s[half * TAPS + tap] = total[:, tap * 128 : tap * 128 + 128]
    used = (rows2 // 16) * TAPS
    for t in range(used, n_gy * per):
        s3s[t] = jnp.zeros((16, 128), BF)

    def stage3(d):
        to = lax.rem(j + d, n_gy)
        return remote(s3s.at[pl.ds(to * per, per)], s3r.at[j], r3_s.at[d], r3_r.at[d], (i, to))

    def stage3_arrival(d):
        frm = lax.rem(j - d + n_gy, n_gy)
        return remote(s3s.at[pl.ds(frm * per, per)], s3r.at[frm], r3_s.at[d], r3_r.at[d], (i, frm))

    for d in range(1, n_gy):
        stage3(d).start()

    lax.fori_loop(6, 8, grad_in, 0)

    for d in range(1, n_gy):
        stage3_arrival(d).wait_recv()
    total = s3s[pl.ds(j * per, per)].astype(F32)
    for d in range(1, n_gy):
        total = total + s3r[lax.rem(j + d, n_gy)].astype(F32)
    ag[core, xq, pl.ds(j * per, per)] = total.astype(BF)

    def stage4(d):
        to = lax.rem(j + d, n_gy)
        here = ag.at[core, xq, pl.ds(j * per, per)]
        return remote(here, here, g4_s.at[d], g4_r.at[d], (i, to))

    def stage4_arrival(d):
        frm = lax.rem(j - d + n_gy, n_gy)
        here = ag.at[core, xq, pl.ds(frm * per, per)]
        return remote(here, here, g4_s.at[d], g4_r.at[d], (i, frm))

    for d in range(1, n_gy):
        stage4(d).start()

    own2.wait()
    for d in range(1, n_gy):
        a2a_arrival(d, outg, arr, a2_s, a2_r).wait_recv()
    for d in range(1, n_gy):
        a2a(d, csend, ret, a1_s, a1_r).wait_send()

    def owned_step(n, carry):
        t, vg = n // 4, n % 4
        rhs = arr[pl.ds(16 * t, 16), pl.ds(pl.multiple_of(16 * vg, 16), 16), :].reshape(256, 256)
        res = dot(pc[0], rhs).astype(BF)
        for v in range(16):
            cv[pl.ds(pl.multiple_of(16 * t, 16), 16), pl.ds(pl.multiple_of(4096 * vg + 256 * v, 256), 256)] = res[16 * v : 16 * v + 16]
        return carry

    lax.fori_loop(0, 12, owned_step, 0)
    owned_copy = pltpu.make_async_copy(cv, owned_out.at[0, 0], sem_out.at[0])
    owned_copy.start()

    for d in range(1, n_gy):
        stage4_arrival(d).wait_recv()

    def stage5(d):
        to = lax.rem(xq + d, n_x)
        here = ag.at[core, xq]
        return remote(here, here, g5_s.at[d], g5_r.at[d], (2 * to + core, j))

    def stage5_arrival(d):
        frm = lax.rem(xq - d + n_x, n_x)
        here = ag.at[core, frm]
        return remote(here, here, g5_s.at[d], g5_r.at[d], (2 * frm + core, j))

    def stage6(d):
        frm = lax.rem(xq - d + n_x, n_x)
        here = ag.at[core, frm]
        return remote(here, here, g6_s.at[d], g6_r.at[d], (sib, j))

    def stage6_arrival(d):
        frm = lax.rem(xq - d + n_x, n_x)
        here = ag.at[1 - core, frm]
        return remote(here, here, g6_s.at[d], g6_r.at[d], (sib, j))

    for d in range(1, n_x):
        stage5(d).start()
    stage6(0).start()
    for d in range(1, n_x):
        stage5_arrival(d).wait_recv()
        stage6(d).start()
    for d in range(n_x):
        stage6_arrival(d).wait_recv()

    scale = float(8 * 8 * 32 * n_gx * n_gy) ** -0.5

    def gw_copy(tap):
        return pltpu.make_async_copy(gws.at[tap], gw_out.at[tap], sem_gw.at[tap])

    def finish(tap, carry):
        rows = jnp.concatenate(
            [
                ag[cc, q, half * TAPS + tap]
                for cc in range(2)
                for q in range(n_x)
                for half in range(rows2 // 16)
            ],
            0,
        )
        gws[tap] = dot_nt(pc[1, 0:128, 0:128], rows) * scale
        gw_copy(tap).start()
        return carry

    lax.fori_loop(0, TAPS, finish, 0)

    for d in range(1, n_gy):
        a2a(d, outg, arr, a2_s, a2_r).wait_send()
        stage3(d).wait_send()
        stage4(d).wait_send()
    for d in range(1, n_x):
        stage2(d).wait_send()
        stage5(d).wait_send()
    for d in range(n_x):
        stage6(d).wait_send()
    owned_copy.wait()
    for x in range(16):
        gin_copy(x).wait()
    for tap in range(TAPS):
        gw_copy(tap).wait()


def on_device(n_gx, n_gy, features, occupancy, weight, owner, cotangent):
    cap = cotangent.shape[2] // n_gy
    n_x = n_gx // 2
    rows2 = 128 // n_x
    per = -(-(rows2 // 16) * TAPS // n_gy)
    slots_n = n_gy * cap
    targets = owner.reshape(-1)
    b = jnp.arange(32, dtype=jnp.int32)
    earlier = (targets[:, None] == targets[None, :]) & (b[:, None] > b[None, :])
    slots = targets * cap + jnp.sum(earlier.astype(jnp.int32), axis=1)
    base = (b // 16) * 64 + b % 16
    hit = jnp.arange(slots_n, dtype=jnp.int32)[:, None] == slots[None, :]
    inv = jnp.sum(jnp.where(hit, base[None, :] + 1, 0), axis=1) - 1

    V = pltpu.VMEM
    D = pltpu.SemaphoreType.DMA
    scratch = [
        V((17, 17, 64, 128), BF),
        V((17, 256, 1152), BF),
        V((16, 4, 256, 128), BF),
        V((8, 256, 128), BF),
        V((128, 16, 256), BF),
        V((slots_n, 16384), BF),
        V((slots_n, 64, 256), BF),
        V((slots_n, 64, 256), BF),
        V((slots_n, 64, 256), BF),
        V((slots_n, 64, 256), BF),
        V((TAPS * 128, 256), BF),
        V((9, 256, 256), BF),
        V((9, 32, 256), BF),
        V((8, 32, 256), BF),
        V((2, 9, 256, 512), BF),
        V((256, 2048), BF),
        V((16, 64, 128), BF),
        V((16, 64, 128), BF),
        V((16, 16, 64, 128), BF),
        V((256, TAPS * 128), F32),
        V((128, TAPS * 128), BF),
        V((128, TAPS * 128), BF),
        V((n_x, rows2, TAPS * 128), BF),
        V((n_x, rows2, TAPS * 128), BF),
        V((n_gy * per, 16, 128), BF),
        V((n_gy, per, 16, 128), BF),
        V((2, n_x, n_gy * per, 16, 128), BF),
        V((TAPS, 128, 256), F32),
        V((4, 128, 256), BF),
        V((2, 256, 256), BF),
        V((256, 256), BF),
        V((4, 256, 256), BF),
        V((128, 128), BF),
        D((16,)), D((2,)), D((2,)), D((1,)), D((16,)), D((TAPS,)),
        D((n_gy,)), D((n_gy,)), D((n_gy,)), D((n_gy,)),
        D((3,)), D((3,)), D((3,)), D((3,)),
        D((3,)), D((3,)), D((n_x,)), D((n_x,)),
        D((n_gy,)), D((n_gy,)), D((n_gy,)), D((n_gy,)),
        D((n_x,)), D((n_x,)), D((n_x,)), D((n_x,)),
    ]

    def body(*refs):
        kernel(n_gx, n_gy, cap, per, *refs)

    return pl.pallas_call(
        body,
        out_shape=(
            jax.ShapeDtypeStruct(cotangent.shape, BF),
            jax.ShapeDtypeStruct(features.shape, BF),
            jax.ShapeDtypeStruct(weight.shape, F32),
        ),
        in_specs=[
            pl.BlockSpec(memory_space=pltpu.SMEM),
            pl.BlockSpec(memory_space=pltpu.SMEM),
            pl.BlockSpec(memory_space=pltpu.VMEM),
            pl.BlockSpec(memory_space=pl.ANY),
            pl.BlockSpec(memory_space=pl.ANY),
            pl.BlockSpec(memory_space=pl.ANY),
        ],
        out_specs=[pl.BlockSpec(memory_space=pl.ANY)] * 3,
        scratch_shapes=scratch,
        compiler_params=pltpu.CompilerParams(
            collective_id=0, has_side_effects=True, vmem_limit_bytes=63 * 1024 * 1024
        ),
        cost_estimate=pl.CostEstimate(
            flops=12_000_000_000, bytes_accessed=20_000_000, transcendentals=0
        ),
    )(slots, inv, occupancy, features, weight.reshape(TAPS * 128, 256), cotangent)


def solution(mesh):
    n_gx, n_gy = mesh.shape["gx"], mesh.shape["gy"]

    def local(*args):
        return on_device(n_gx, n_gy, *args)

    in_specs = (
        P("gx", "gy", None, None),
        P("gx", "gy", None),
        P(),
        P("gx", "gy", None),
        P("gx", "gy", None, None),
    )
    out_specs = (P("gx", "gy", None, None), P("gx", "gy", None, None), P())
    return jax.shard_map(
        local, mesh=mesh, in_specs=in_specs, out_specs=out_specs, check_vma=False
    )
```

profile of v0, /device:TPU:1, one launch (start us, length us, event | category | flops | bytes accessed | tf_op | source)
XLA Modules:
  0.0 137.3 jit_solution(4629432846824842990)
XLA Ops:
  0.6 0.9 convert_reduce_fusion
  1.5 0.7 fusion.2
  2.2 0.0 copy-start.1
  2.2 0.1 select_reduce_fusion
  2.3 0.5 broadcast_add_fusion.refs_1_
  2.8 0.0 copy-done.1
  2.8 124.3 %shard_map.76 = (bf16[1,1,48,16384]{3,2,1,0:T(8,128)(2,1)}, bf16[16,16,64,128]{3,2,1,0:T(8,128)(2,1)}, f32[27,128,256]{2,1,0:T(8,128)}) custom-call(s32[32]{0:T(128)} %copy-done.1, s32[48]{0:T(128)} %broadcast_add_fusion.refs_1_, s32[16,16,64]{2,1,0:T(8,128)} %refs_2_.1, bf16[16,16,64,128]{3,2,1,0:T(8,128)(2,1)} %refs_3_.1, bf16[3456,256]{1,0:T(8,128)(2,1)} %bitcast.4, ...), custom_call_target="tpu_custom_call" | custom-call | flops 12000000000 | bytes 20000000 | tf_op jit(solution)/shard_map/pallas_call | solution.py:597
  127.2 2.7 %copy.11 = bf16[1,1,48,16384]{3,2,1,0:T(8,128)(2,1)} copy(bf16[1,1,48,16384]{3,2,1,0:T(8,128)(2,1)} %get-tuple-element.8) | data formatting | bytes 3145728
  129.8 0.0 copy-start
  129.8 5.7 %copy.12 = bf16[16,16,64,128]{3,2,1,0:T(8,128)(2,1)} copy(bf16[16,16,64,128]{3,2,1,0:T(8,128)(2,1)} %get-tuple-element.9) | data formatting | bytes 8388608
  135.5 0.0 copy-done
  135.5 1.8 %copy.13 = f32[27,128,256]{2,1,0:T(8,128)} copy(f32[27,128,256]{2,1,0:T(8,128)S(1)} %copy-done) | data formatting | bytes 7077888
Async XLA Ops:
  2.2 0.6 copy-start.1
  129.8 5.7 %copy-start = (f32[27,128,256]{2,1,0:T(8,128)S(1)}, f32[27,128,256]{2,1,0:T(8,128)}, u32[]{:S(2)}) copy-start(f32[27,128,256]{2,1,0:T(8,128)} %get-tuple-element.10) | copy-start | bytes 10616836
where the time goes:
time: 137 us
  Pallas kernels  124 us (91%)
  local copies, waits for them, and re-layouts  10.1 us (7%)
  other arithmetic  2.18 us (2%)
    pallas_call x1, Pallas kernels, on_device(): pl.pallas_call(body, out_shape=(jax.ShapeDtypeStruct(cotangent.shape, BF)...  124 us
    unnamed x7, local copies, waits for them, and re-layouts  10.1 us

commit v1 on v0

--- a/solution.py
+++ b/solution.py
@@ -9,7 +9,8 @@
 F32 = jnp.float32
 MESH = pl.DeviceIdType.MESH
 TAPS = 27
-TILES = 54
+CHUNKS = ((0, 8), (8, 16), (16, 27))
+FAR_FIRST = (10, 6, 9, 11, 14, 5, 7, 13, 15, 2, 8, 1, 3, 4, 12)
 
 
 def iota2(shape, dim):
@@ -28,17 +29,44 @@
     return lax.dot_general(a, b, (((1,), (1,)), ((), ())), preferred_element_type=F32)
 
 
+def chunk_plan(n_x, n_gy):
+    halves = 128 // n_x // 16
+    plan, first, mine = [], 0, 0
+    for t0, t1 in CHUNKS:
+        used = halves * (t1 - t0)
+        per = -(-used // n_gy)
+        plan.append((used, per, first, mine))
+        first += per * n_gy
+        mine += per
+    return plan, first, mine
+
+
+def tile_of(plan, half, tap):
+    for (t0, t1), (_, _, first, _) in zip(CHUNKS, plan):
+        if t0 <= tap < t1:
+            return first + half * (t1 - t0) + tap - t0
+
+
+def partner(j, d):
+    total, bit = 0, 1
+    while bit <= 8:
+        b = (j // bit) % 2
+        total = total + bit * (1 - b if d & bit else b)
+        bit *= 2
+    return total
+
+
 def row_coords(rows):
     return rows // 128, (rows // 16) % 8, (rows // 4) % 4, rows % 4
 
 
 def kernel(
-    n_gx, n_gy, cap, per,
+    n_gx, n_gy, cap,
     slot_ref, inv_ref, occ_ref, feat, weight, cot,
-    owned_out, gin_out, gw_out,
+    ov, gi, ag,
     fp, pt, mk, act, bk, cv, csend, ret, outg, arr, wv, ub, yhu, ysu, uu, upt,
-    xs, ys, gi, dwf, s1s, s1r, s2s, s2r, s3s, s3r, ag, gws, pk, pc, po, qs, pysel,
-    sem_feat, sem_in, sem_loc, sem_out, sem_gi, sem_gw,
+    xs, ys, dwf, s1s, s1r, s2s, s2r, s3s, s3r, pk, pc, po, qs, pysel,
+    sem_feat, sem_in, sem_loc,
     a1_s, a1_r, a2_s, a2_r, h_s, h_r, u_s, u_r,
     r1_s, r1_r, r2_s, r2_r, r3_s, r3_r, g4_s, g4_r, g5_s, g5_r, g6_s, g6_r,
 ):
@@ -63,7 +91,9 @@
     w_copy.start()
 
     barrier = pltpu.get_barrier_semaphore()
-    peers = [(i, lax.rem(j + d, n_gy)) for d in range(1, n_gy)]
+    order = [d for d in FAR_FIRST if d < n_gy]
+    peer_j = {d: partner(j, d) for d in order}
+    peers = [(i, peer_j[d]) for d in order]
     peers += [(lax.rem(i + d, n_gx), j) for d in range(2, n_gx - 1, 2)]
     peers += [(nxt_i, j), (prv_i, j), (nxt_i, nxt_j), (prv_i, prv_j)]
     for peer in peers:
@@ -96,8 +126,6 @@
     _, cbz, cvy, cvz = row_coords(c)
     pysel[...] = as_bf((r < 32) & (cvy == 0) & (4 * cbz + cvz == r))
 
-    pl.semaphore_wait(barrier, len(peers))
-
     cot_copy.wait()
 
     def cot_step(n, carry):
@@ -115,34 +143,22 @@
 
     lax.fori_loop(0, 12, cot_step, 0)
 
+    def remote(src, dst, s_sem, r_sem, to):
+        return pltpu.make_async_remote_copy(
+            src_ref=src, dst_ref=dst, send_sem=s_sem, recv_sem=r_sem,
+            device_id=to, device_id_type=MESH,
+        )
+
     def a2a(d, src, dst, s_sem, r_sem):
-        to = lax.rem(j + d, n_gy)
-        return pltpu.make_async_remote_copy(
-            src_ref=src.at[pl.ds(to * cap, cap)],
-            dst_ref=dst.at[pl.ds(j * cap, cap)],
-            send_sem=s_sem.at[d],
-            recv_sem=r_sem.at[d],
-            device_id=(i, to),
-            device_id_type=MESH,
+        to = peer_j[d]
+        return remote(
+            src.at[pl.ds(to * cap, cap)], dst.at[pl.ds(j * cap, cap)], s_sem.at[d], r_sem.at[d], (i, to)
         )
 
     def a2a_arrival(d, src, dst, s_sem, r_sem):
-        frm = lax.rem(j - d + n_gy, n_gy)
-        return pltpu.make_async_remote_copy(
-            src_ref=src.at[pl.ds(frm * cap, cap)],
-            dst_ref=dst.at[pl.ds(frm * cap, cap)],
-            send_sem=s_sem.at[d],
-            recv_sem=r_sem.at[d],
-            device_id=(i, frm),
-            device_id_type=MESH,
-        )
-
-    for d in range(1, n_gy):
-        a2a(d, csend, ret, a1_s, a1_r).start()
-    own1 = pltpu.make_async_copy(
-        csend.at[pl.ds(j * cap, cap)], ret.at[pl.ds(j * cap, cap)], sem_loc.at[0]
-    )
-    own1.start()
+        frm = peer_j[d]
+        here = pl.ds(frm * cap, cap)
+        return remote(src.at[here], dst.at[here], s_sem.at[d], r_sem.at[d], (i, frm))
 
     def occ_row(x, y):
         return occ_ref[x, pl.ds(y, 1), :].astype(F32)
@@ -167,14 +183,6 @@
             for v in range(4):
                 xs[8 * by + 2 * v + py] = res[64 * v : 64 * v + 64]
 
-    def remote(src, dst, s_sem, r_sem, to):
-        return pltpu.make_async_remote_copy(
-            src_ref=src, dst_ref=dst, send_sem=s_sem, recv_sem=r_sem,
-            device_id=to, device_id_type=MESH,
-        )
-
-    halo_x = remote(xs, fp.at[0, pl.ds(1, 16)], h_s.at[0], h_r.at[0], (nxt_i, j))
-    halo_x.start()
     for x in range(14, -1, -1):
         feat_copy(x).wait()
 
@@ -185,10 +193,19 @@
         return carry
 
     lax.fori_loop(0, 16, mask_y, 0)
+    pl.semaphore_wait(barrier, len(peers))
+    halo_x = remote(xs, fp.at[0, pl.ds(1, 16)], h_s.at[0], h_r.at[0], (nxt_i, j))
     halo_y = remote(ys, fp.at[pl.ds(1, 16), 0], h_s.at[1], h_r.at[1], (i, nxt_j))
+    halo_c = remote(ys.at[15], fp.at[0, 0], h_s.at[2], h_r.at[2], (nxt_i, nxt_j))
     halo_y.start()
-    halo_c = remote(ys.at[15], fp.at[0, 0], h_s.at[2], h_r.at[2], (nxt_i, nxt_j))
+    halo_x.start()
     halo_c.start()
+    for d in order:
+        a2a(d, csend, ret, a1_s, a1_r).start()
+    own1 = pltpu.make_async_copy(
+        csend.at[pl.ds(j * cap, cap)], ret.at[pl.ds(j * cap, cap)], sem_loc.at[0]
+    )
+    own1.start()
 
     ones = jnp.ones((256, 128), F32).astype(BF)
 
@@ -266,14 +283,8 @@
     lax.fori_loop(0, n_gy * cap, pack, 0)
 
     own1.wait()
-    for d in range(1, n_gy):
+    for d in order:
         a2a_arrival(d, csend, ret, a1_s, a1_r).wait_recv()
-    for d in range(1, n_gy):
-        a2a(d, outg, arr, a2_s, a2_r).start()
-    own2 = pltpu.make_async_copy(
-        outg.at[pl.ds(j * cap, cap)], arr.at[pl.ds(j * cap, cap)], sem_loc.at[1]
-    )
-    own2.start()
 
     def place(b, carry):
         s = slot_ref[b]
@@ -296,26 +307,161 @@
     up_y.start()
     up_c.start()
 
+    for d in order:
+        a2a(d, outg, arr, a2_s, a2_r).start()
+    own2 = pltpu.make_async_copy(
+        outg.at[pl.ds(j * cap, cap)], arr.at[pl.ds(j * cap, cap)], sem_loc.at[1]
+    )
+    own2.start()
+
     for ox in range(8):
         upt[:, ox * 256 : ox * 256 + 256] = dot_nt(pc[1], ub[ox]).astype(BF)
 
     mine = pl.multiple_of(core * 128, 128)
     other = pl.multiple_of(128 - core * 128, 128)
 
-    def stage1(kx):
-        cols = pl.ds(kx * 1152, 1152)
-        return remote(s1s.at[:, cols], s1r.at[:, cols], r1_s.at[kx], r1_r.at[kx], (sib, j))
-
-    for kx in range(3):
-        for n in range(5):
-            width = 256 if n < 4 else 128
-            rhs = jnp.concatenate(
-                [pt[2 * ox + kx, :, n * 256 : n * 256 + width] for ox in range(8)], 0
-            )
-            col = kx * 1152 + n * 256
-            dwf[:, col : col + width] = dot(upt[...], rhs)
-        s1s[:, kx * 1152 : kx * 1152 + 1152] = dwf[pl.ds(other, 128), kx * 1152 : kx * 1152 + 1152].astype(BF)
-        stage1(kx).start()
+    rows2 = 128 // n_x
+    plan, _, _ = chunk_plan(n_x, n_gy)
+
+    def columns(n):
+        return slice(CHUNKS[n][0] * 128, CHUNKS[n][1] * 128)
+
+    def tap_rows(tap):
+        kx, col = tap // 9, (tap % 9) * 128
+        return jnp.concatenate([pt[2 * ox + kx, :, col : col + 128] for ox in range(8)], 0)
+
+    def stage1(n):
+        cols = columns(n)
+        return remote(s1s.at[:, cols], s1r.at[:, cols], r1_s.at[n], r1_r.at[n], (sib, j))
+
+    def weight_chunk(n):
+        t0, t1 = CHUNKS[n]
+        for tap in range(t0, t1, 2):
+            rhs = tap_rows(tap)
+            if tap + 1 < t1:
+                rhs = jnp.concatenate([rhs, tap_rows(tap + 1)], 1)
+            dwf[:, tap * 128 : tap * 128 + rhs.shape[1]] = dot(upt[...], rhs)
+        cols = columns(n)
+        s1s[:, cols] = dwf[pl.ds(other, 128), cols].astype(BF)
+        stage1(n).start()
+
+    def stage2(n, d):
+        cols = columns(n)
+        to = lax.rem(xq + d, n_x)
+        return remote(s2s.at[to, :, cols], s2r.at[xq, :, cols], r2_s.at[n, d], r2_r.at[n, d], (2 * to + core, j))
+
+    def stage2_arrival(n, d):
+        cols = columns(n)
+        frm = lax.rem(xq - d + n_x, n_x)
+        return remote(s2s.at[frm, :, cols], s2r.at[frm, :, cols], r2_s.at[n, d], r2_r.at[n, d], (2 * frm + core, j))
+
+    def after1(n):
+        cols = columns(n)
+        stage1(n).wait()
+        for q in range(n_x):
+            at = pl.multiple_of(mine + q * rows2, 16)
+            mid = dwf[pl.ds(at, rows2), cols] + s1r[q * rows2 : (q + 1) * rows2, cols].astype(F32)
+            dwf[pl.ds(at, rows2), cols] = mid
+            s2s[q, :, cols] = mid.astype(BF)
+        for d in range(1, n_x):
+            stage2(n, d).start()
+
+    def stage3(n, d):
+        _, per, first, own = plan[n]
+        to = peer_j[d]
+        return remote(
+            s3s.at[pl.ds(first + to * per, per)], s3r.at[j, pl.ds(own, per)],
+            r3_s.at[n, d], r3_r.at[n, d], (i, to),
+        )
+
+    def stage3_arrival(n, d):
+        _, per, first, own = plan[n]
+        frm = peer_j[d]
+        return remote(
+            s3s.at[pl.ds(first + frm * per, per)], s3r.at[frm, pl.ds(own, per)],
+            r3_s.at[n, d], r3_r.at[n, d], (i, frm),
+        )
+
+    def after2(n):
+        used, per, first, _ = plan[n]
+        t0, t1 = CHUNKS[n]
+        cols = columns(n)
+        for d in range(1, n_x):
+            stage2_arrival(n, d).wait_recv()
+        for half in range(rows2 // 16):
+            at = pl.multiple_of(mine + xq * rows2 + half * 16, 16)
+            total = dwf[pl.ds(at, 16), cols]
+            for d in range(1, n_x):
+                frm = lax.rem(xq + d, n_x)
+                total = total + s2r[frm, half * 16 : half * 16 + 16, cols].astype(F32)
+            total = total.astype(BF)
+            for t in range(t1 - t0):
+                s3s[first + half * (t1 - t0) + t] = total[:, t * 128 : t * 128 + 128]
+        for t in range(first + used, first + per * n_gy):
+            s3s[t] = jnp.zeros((16, 128), BF)
+        for d in order:
+            stage3(n, d).start()
+
+    def stage4(n, d):
+        _, per, first, _ = plan[n]
+        here = ag.at[core, xq, pl.ds(first + j * per, per)]
+        return remote(here, here, g4_s.at[n, d], g4_r.at[n, d], (i, peer_j[d]))
+
+    def stage4_arrival(n, d):
+        _, per, first, _ = plan[n]
+        here = ag.at[core, xq, pl.ds(first + peer_j[d] * per, per)]
+        return remote(here, here, g4_s.at[n, d], g4_r.at[n, d], (i, peer_j[d]))
+
+    def after3(n):
+        _, per, first, own = plan[n]
+        for d in order:
+            stage3_arrival(n, d).wait_recv()
+        total = s3s[pl.ds(first + j * per, per)].astype(F32)
+        for d in order:
+            total = total + s3r[peer_j[d], own : own + per].astype(F32)
+        ag[core, xq, pl.ds(first + j * per, per)] = total.astype(BF)
+        for d in order:
+            stage4(n, d).start()
+
+    def block(c, q, n):
+        used, _, first, _ = plan[n]
+        return ag.at[c, q, first : first + used]
+
+    def stage5(n, d):
+        to = lax.rem(xq + d, n_x)
+        here = block(core, xq, n)
+        return remote(here, here, g5_s.at[n, d], g5_r.at[n, d], (2 * to + core, j))
+
+    def stage5_arrival(n, d):
+        frm = lax.rem(xq - d + n_x, n_x)
+        here = block(core, frm, n)
+        return remote(here, here, g5_s.at[n, d], g5_r.at[n, d], (2 * frm + core, j))
+
+    def stage6(n, d):
+        here = block(core, lax.rem(xq - d + n_x, n_x), n)
+        return remote(here, here, g6_s.at[n, d], g6_r.at[n, d], (sib, j))
+
+    def stage6_arrival(n, d):
+        here = block(1 - core, lax.rem(xq - d + n_x, n_x), n)
+        return remote(here, here, g6_s.at[n, d], g6_r.at[n, d], (sib, j))
+
+    def after4(n):
+        for d in order:
+            stage4_arrival(n, d).wait_recv()
+        for d in range(1, n_x):
+            stage5(n, d).start()
+        stage6(n, 0).start()
+
+    def after5(n):
+        for d in range(1, n_x):
+            stage5_arrival(n, d).wait_recv()
+            stage6(n, d).start()
+
+    weight_chunk(0)
+    weight_chunk(1)
+    after1(0)
+    weight_chunk(2)
+    after1(1)
 
     up_x.wait()
     up_y.wait()
@@ -337,9 +483,6 @@
     lax.fori_loop(0, 9, shifts, 0)
 
     lists = (((1, 0),), ((2, 0), (0, 1)))
-
-    def gin_copy(x):
-        return pltpu.make_async_copy(gi.at[x], gin_out.at[x], sem_gi.at[x])
 
     def grad_in(ox, carry):
         for px in range(2):
@@ -367,177 +510,94 @@
                 for by in range(2):
                     for v in range(4):
                         gi[2 * ox + px, 8 * by + 2 * v + py] = res[64 * v : 64 * v + 64, 128 * by : 128 * by + 128]
-            gin_copy(2 * ox + px).start()
-        return carry
-
-    lax.fori_loop(0, 2, grad_in, 0)
-
-    def stage2(d):
-        to = lax.rem(xq + d, n_x)
-        return remote(s2s.at[to], s2r.at[xq], r2_s.at[d], r2_r.at[d], (2 * to + core, j))
-
-    def stage2_arrival(d):
-        frm = lax.rem(xq - d + n_x, n_x)
-        return remote(s2s.at[frm], s2r.at[frm], r2_s.at[d], r2_r.at[d], (2 * frm + core, j))
-
-    for kx in range(3):
-        stage1(kx).wait()
-
-    def sum1(q, carry):
-        at = pl.multiple_of(mine + q * s2s.shape[1], 16)
-        rows = s2s.shape[1]
-        mid = dwf[pl.ds(at, rows), :] + s1r[pl.ds(pl.multiple_of(q * rows, 16), rows), :].astype(F32)
-        dwf[pl.ds(at, rows), :] = mid
-        s2s[q] = mid.astype(BF)
-        return carry
-
-    lax.fori_loop(0, n_x, sum1, 0)
-    for d in range(1, n_x):
-        stage2(d).start()
-
-    lax.fori_loop(2, 6, grad_in, 0)
-
-    for d in range(1, n_x):
-        stage2_arrival(d).wait_recv()
-    rows2 = s2s.shape[1]
-    for half in range(rows2 // 16):
-        at = pl.multiple_of(mine + xq * rows2 + half * 16, 16)
-        total = dwf[pl.ds(at, 16), :]
-        for d in range(1, n_x):
-            frm = lax.rem(xq + d, n_x)
-            total = total + s2r[frm, half * 16 : half * 16 + 16, :].astype(F32)
-        total = total.astype(BF)
-        for tap in range(TAPS):
-            s3s[half * TAPS + tap] = total[:, tap * 128 : tap * 128 + 128]
-    used = (rows2 // 16) * TAPS
-    for t in range(used, n_gy * per):
-        s3s[t] = jnp.zeros((16, 128), BF)
-
-    def stage3(d):
-        to = lax.rem(j + d, n_gy)
-        return remote(s3s.at[pl.ds(to * per, per)], s3r.at[j], r3_s.at[d], r3_r.at[d], (i, to))
-
-    def stage3_arrival(d):
-        frm = lax.rem(j - d + n_gy, n_gy)
-        return remote(s3s.at[pl.ds(frm * per, per)], s3r.at[frm], r3_s.at[d], r3_r.at[d], (i, frm))
-
-    for d in range(1, n_gy):
-        stage3(d).start()
-
-    lax.fori_loop(6, 8, grad_in, 0)
-
-    for d in range(1, n_gy):
-        stage3_arrival(d).wait_recv()
-    total = s3s[pl.ds(j * per, per)].astype(F32)
-    for d in range(1, n_gy):
-        total = total + s3r[lax.rem(j + d, n_gy)].astype(F32)
-    ag[core, xq, pl.ds(j * per, per)] = total.astype(BF)
-
-    def stage4(d):
-        to = lax.rem(j + d, n_gy)
-        here = ag.at[core, xq, pl.ds(j * per, per)]
-        return remote(here, here, g4_s.at[d], g4_r.at[d], (i, to))
-
-    def stage4_arrival(d):
-        frm = lax.rem(j - d + n_gy, n_gy)
-        here = ag.at[core, xq, pl.ds(frm * per, per)]
-        return remote(here, here, g4_s.at[d], g4_r.at[d], (i, frm))
-
-    for d in range(1, n_gy):
-        stage4(d).start()
+        return carry
+
+    def grads(lo, hi):
+        lax.fori_loop(lo, hi, grad_in, 0)
+
+    after1(2)
+    grads(0, 1)
+    after2(0)
+    grads(1, 2)
+    after2(1)
+    after3(0)
+    grads(2, 3)
+    after2(2)
+    after3(1)
+    grads(3, 4)
+    after4(0)
+    after3(2)
+    grads(4, 5)
+    after4(1)
+    grads(5, 6)
+    after5(0)
+    after4(2)
+    grads(6, 8)
+    after5(1)
 
     own2.wait()
-    for d in range(1, n_gy):
+    for d in order:
         a2a_arrival(d, outg, arr, a2_s, a2_r).wait_recv()
-    for d in range(1, n_gy):
-        a2a(d, csend, ret, a1_s, a1_r).wait_send()
 
     def owned_step(n, carry):
         t, vg = n // 4, n % 4
         rhs = arr[pl.ds(16 * t, 16), pl.ds(pl.multiple_of(16 * vg, 16), 16), :].reshape(256, 256)
         res = dot(pc[0], rhs).astype(BF)
         for v in range(16):
-            cv[pl.ds(pl.multiple_of(16 * t, 16), 16), pl.ds(pl.multiple_of(4096 * vg + 256 * v, 256), 256)] = res[16 * v : 16 * v + 16]
+            ov[pl.ds(pl.multiple_of(16 * t, 16), 16), pl.ds(pl.multiple_of(4096 * vg + 256 * v, 256), 256)] = res[16 * v : 16 * v + 16]
         return carry
 
     lax.fori_loop(0, 12, owned_step, 0)
-    owned_copy = pltpu.make_async_copy(cv, owned_out.at[0, 0], sem_out.at[0])
-    owned_copy.start()
-
-    for d in range(1, n_gy):
-        stage4_arrival(d).wait_recv()
-
-    def stage5(d):
-        to = lax.rem(xq + d, n_x)
-        here = ag.at[core, xq]
-        return remote(here, here, g5_s.at[d], g5_r.at[d], (2 * to + core, j))
-
-    def stage5_arrival(d):
-        frm = lax.rem(xq - d + n_x, n_x)
-        here = ag.at[core, frm]
-        return remote(here, here, g5_s.at[d], g5_r.at[d], (2 * frm + core, j))
-
-    def stage6(d):
-        frm = lax.rem(xq - d + n_x, n_x)
-        here = ag.at[core, frm]
-        return remote(here, here, g6_s.at[d], g6_r.at[d], (sib, j))
-
-    def stage6_arrival(d):
-        frm = lax.rem(xq - d + n_x, n_x)
-        here = ag.at[1 - core, frm]
-        return remote(here, here, g6_s.at[d], g6_r.at[d], (sib, j))
-
-    for d in range(1, n_x):
-        stage5(d).start()
-    stage6(0).start()
-    for d in range(1, n_x):
-        stage5_arrival(d).wait_recv()
-        stage6(d).start()
-    for d in range(n_x):
-        stage6_arrival(d).wait_recv()
-
-    scale = float(8 * 8 * 32 * n_gx * n_gy) ** -0.5
-
-    def gw_copy(tap):
-        return pltpu.make_async_copy(gws.at[tap], gw_out.at[tap], sem_gw.at[tap])
-
-    def finish(tap, carry):
+
+    after5(2)
+    for n in range(len(CHUNKS)):
+        for d in range(n_x):
+            stage6_arrival(n, d).wait_recv()
+
+    for d in order:
+        a2a(d, csend, ret, a1_s, a1_r).wait_send()
+        a2a(d, outg, arr, a2_s, a2_r).wait_send()
+    for n in range(len(CHUNKS)):
+        for d in order:
+            stage3(n, d).wait_send()
+            stage4(n, d).wait_send()
+        for d in range(1, n_x):
+            stage2(n, d).wait_send()
+            stage5(n, d).wait_send()
+        for d in range(n_x):
+            stage6(n, d).wait_send()
+
+
+def finish_kernel(n_x, n_gy, scale, ov, gi, ag, owned_out, gin_out, gw_out, gws, sem_big, sem_gw):
+    plan, _, _ = chunk_plan(n_x, n_gy)
+    copies = [pltpu.make_async_copy(gi.at[pl.ds(4 * n, 4)], gin_out.at[pl.ds(4 * n, 4)], sem_big.at[n]) for n in range(4)]
+    copies.append(pltpu.make_async_copy(ov, owned_out, sem_big.at[4]))
+    for copy in copies:
+        copy.start()
+    eye = as_bf(iota2((128, 128), 0) == iota2((128, 128), 1))
+    for tap in range(TAPS):
         rows = jnp.concatenate(
             [
-                ag[cc, q, half * TAPS + tap]
-                for cc in range(2)
+                ag[c, q, tile_of(plan, half, tap)]
+                for c in range(2)
                 for q in range(n_x)
-                for half in range(rows2 // 16)
+                for half in range(128 // n_x // 16)
             ],
             0,
         )
-        gws[tap] = dot_nt(pc[1, 0:128, 0:128], rows) * scale
-        gw_copy(tap).start()
-        return carry
-
-    lax.fori_loop(0, TAPS, finish, 0)
-
-    for d in range(1, n_gy):
-        a2a(d, outg, arr, a2_s, a2_r).wait_send()
-        stage3(d).wait_send()
-        stage4(d).wait_send()
-    for d in range(1, n_x):
-        stage2(d).wait_send()
-        stage5(d).wait_send()
-    for d in range(n_x):
-        stage6(d).wait_send()
-    owned_copy.wait()
-    for x in range(16):
-        gin_copy(x).wait()
-    for tap in range(TAPS):
-        gw_copy(tap).wait()
+        gws[tap] = dot_nt(eye, rows) * scale
+        copy = pltpu.make_async_copy(gws.at[tap], gw_out.at[tap], sem_gw.at[tap])
+        copy.start()
+        copies.append(copy)
+    for copy in copies:
+        copy.wait()
 
 
 def on_device(n_gx, n_gy, features, occupancy, weight, owner, cotangent):
     cap = cotangent.shape[2] // n_gy
     n_x = n_gx // 2
     rows2 = 128 // n_x
-    per = -(-(rows2 // 16) * TAPS // n_gy)
+    _, tiles, per = chunk_plan(n_x, n_gy)
     slots_n = n_gy * cap
     targets = owner.reshape(-1)
     b = jnp.arange(32, dtype=jnp.int32)
@@ -549,6 +609,7 @@
 
     V = pltpu.VMEM
     D = pltpu.SemaphoreType.DMA
+    nc = len(CHUNKS)
     scratch = [
         V((17, 17, 64, 128), BF),
         V((17, 256, 1152), BF),
@@ -568,56 +629,67 @@
         V((256, 2048), BF),
         V((16, 64, 128), BF),
         V((16, 64, 128), BF),
-        V((16, 16, 64, 128), BF),
         V((256, TAPS * 128), F32),
         V((128, TAPS * 128), BF),
         V((128, TAPS * 128), BF),
         V((n_x, rows2, TAPS * 128), BF),
         V((n_x, rows2, TAPS * 128), BF),
-        V((n_gy * per, 16, 128), BF),
+        V((tiles, 16, 128), BF),
         V((n_gy, per, 16, 128), BF),
-        V((2, n_x, n_gy * per, 16, 128), BF),
-        V((TAPS, 128, 256), F32),
         V((4, 128, 256), BF),
         V((2, 256, 256), BF),
         V((256, 256), BF),
         V((4, 256, 256), BF),
         V((128, 128), BF),
-        D((16,)), D((2,)), D((2,)), D((1,)), D((16,)), D((TAPS,)),
-        D((n_gy,)), D((n_gy,)), D((n_gy,)), D((n_gy,)),
+        D((16,)), D((2,)), D((2,)),
+        D((16,)), D((16,)), D((16,)), D((16,)),
         D((3,)), D((3,)), D((3,)), D((3,)),
-        D((3,)), D((3,)), D((n_x,)), D((n_x,)),
-        D((n_gy,)), D((n_gy,)), D((n_gy,)), D((n_gy,)),
-        D((n_x,)), D((n_x,)), D((n_x,)), D((n_x,)),
+        D((nc,)), D((nc,)), D((nc, n_x)), D((nc, n_x)),
+        D((nc, 16)), D((nc, 16)), D((nc, 16)), D((nc, 16)),
+        D((nc, n_x)), D((nc, n_x)), D((nc, n_x)), D((nc, n_x)),
     ]
 
     def body(*refs):
-        kernel(n_gx, n_gy, cap, per, *refs)
-
-    return pl.pallas_call(
+        kernel(n_gx, n_gy, cap, *refs)
+
+    def finish(*refs):
+        finish_kernel(n_x, n_gy, float(8 * 8 * 32 * n_gx * n_gy) ** -0.5, *refs)
+
+    smem = pl.BlockSpec(memory_space=pltpu.SMEM)
+    vmem = pl.BlockSpec(memory_space=pltpu.VMEM)
+    anywhere = pl.BlockSpec(memory_space=pl.ANY)
+    parts = pl.pallas_call(
         body,
         out_shape=(
-            jax.ShapeDtypeStruct(cotangent.shape, BF),
-            jax.ShapeDtypeStruct(features.shape, BF),
-            jax.ShapeDtypeStruct(weight.shape, F32),
+            V((slots_n, 16384), BF),
+            V((16, 16, 64, 128), BF),
+            V((2, n_x, tiles, 16, 128), BF),
         ),
-        in_specs=[
-            pl.BlockSpec(memory_space=pltpu.SMEM),
-            pl.BlockSpec(memory_space=pltpu.SMEM),
-            pl.BlockSpec(memory_space=pltpu.VMEM),
-            pl.BlockSpec(memory_space=pl.ANY),
-            pl.BlockSpec(memory_space=pl.ANY),
-            pl.BlockSpec(memory_space=pl.ANY),
-        ],
-        out_specs=[pl.BlockSpec(memory_space=pl.ANY)] * 3,
+        in_specs=[smem, smem, vmem, anywhere, anywhere, anywhere],
+        out_specs=[vmem] * 3,
         scratch_shapes=scratch,
         compiler_params=pltpu.CompilerParams(
-            collective_id=0, has_side_effects=True, vmem_limit_bytes=63 * 1024 * 1024
+            collective_id=0, has_side_effects=True, vmem_limit_bytes=50 * 1024 * 1024
         ),
         cost_estimate=pl.CostEstimate(
             flops=12_000_000_000, bytes_accessed=20_000_000, transcendentals=0
         ),
     )(slots, inv, occupancy, features, weight.reshape(TAPS * 128, 256), cotangent)
+    parts = [pltpu.with_memory_space_constraint(part, pltpu.VMEM) for part in parts]
+    owned, gin, gw = pl.pallas_call(
+        finish,
+        out_shape=(
+            jax.ShapeDtypeStruct((slots_n, 16384), BF),
+            jax.ShapeDtypeStruct(features.shape, BF),
+            jax.ShapeDtypeStruct(weight.shape, F32),
+        ),
+        in_specs=[vmem] * 3,
+        out_specs=[anywhere] * 3,
+        scratch_shapes=[V(weight.shape, F32), D((5,)), D((TAPS,))],
+        compiler_params=pltpu.CompilerParams(vmem_limit_bytes=10 * 1024 * 1024),
+        cost_estimate=pl.CostEstimate(flops=500_000_000, bytes_accessed=10_000_000, transcendentals=0),
+    )(*parts)
+    return owned.reshape(cotangent.shape), gin, gw
 
 
 def solution(mesh):

time: 137 us -> 98.5 us (0.72)
  Pallas kernels: 124 us -> 95.3 us
  local copies, waits for them, and re-layouts: 10.1 us -> 0.01 us
    pallas_call x1 -> x2, Pallas kernels: 124 us -> 95.3 us  [the longest x1 91.3 us: on_device(): pl.pallas_call(body, out_shape=(V((slots_n, 16384), BF), V((16, 16, 64, 1...]
    unnamed x7 -> x2, local copies, waits for them, and re-layouts: 10.1 us -> 0.01 us
where the time goes in v1:
time: 98.5 us; the launch traced here: 98.3 us
  Pallas kernels  95.3 us (97%)
  other arithmetic  2.18 us (2%)
    pallas_call x1, Pallas kernels, on_device(): pl.pallas_call(body, out_shape=(V((slots_n, 16384), BF), V((16, 16, 64, 1...  91.3 us
    pallas_call x1, Pallas kernels, on_device(): pl.pallas_call(finish, out_shape=(jax.ShapeDtypeStruct((slots_n, 16384),...  4.02 us

profile of v1, /device:TPU:1, one launch (start us, length us, event | category | flops | bytes accessed | tf_op | source)
XLA Modules:
  0.0 98.3 jit_solution(369689163730725497)
XLA Ops:
  0.6 0.9 convert_reduce_fusion
  1.5 0.7 fusion.2
  2.2 0.0 copy-start
  2.2 0.1 select_reduce_fusion
  2.3 0.5 broadcast_add_fusion.refs_1_
  2.8 0.0 copy-done
  2.8 91.3 %shard_map.76 = (bf16[48,16384]{1,0:T(8,128)(2,1)S(1)}, bf16[16,16,64,128]{3,2,1,0:T(8,128)(2,1)S(1)}, bf16[2,4,64,16,128]{4,3,2,1,0:T(8,128)(2,1)S(1)}) custom-call(s32[32]{0:T(128)} %copy-done, s32[48]{0:T(128)} %broadcast_add_fusion.refs_1_, s32[16,16,64]{2,1,0:T(8,128)} %refs_2_.1, bf16[16,16,64,128]{3,2,1,0:T(8,128)(2,1)} %refs_3_.1, ...), custom_call_target="tpu_custom_call" | custom-call | flops 12000000000 | bytes 20000000 | tf_op jit(solution)/shard_map/pallas_call | solution.py:661
  94.2 4.0 %shard_map.77 = (bf16[48,16384]{1,0:T(8,128)(2,1)}, bf16[16,16,64,128]{3,2,1,0:T(8,128)(2,1)}, f32[27,128,256]{2,1,0:T(8,128)}) custom-call(bf16[48,16384]{1,0:T(8,128)(2,1)S(1)} %get-tuple-element.9.refs_0_, bf16[16,16,64,128]{3,2,1,0:T(8,128)(2,1)S(1)} %get-tuple-element.10.refs_1_, bf16[2,4,64,16,128]{4,3,2,1,0:T(8,128)(2,1)S(1)} %get-tuple-element.11.refs_2_), custom_call_target="tpu_custom_call" | custom-call | flops 500000000 | bytes 10000000 | tf_op jit(solution)/shard_map/pallas_call | solution.py:679
Async XLA Ops:
  2.2 0.6 copy-start

commit v2 on v1

--- a/solution.py
+++ b/solution.py
@@ -10,6 +10,14 @@
 MESH = pl.DeviceIdType.MESH
 TAPS = 27
 CHUNKS = ((0, 8), (8, 16), (16, 27))
+SCHEDULE = (
+    ("send", 0), ("weight", 0), ("weight", 1), ("sum1", 0), ("weight", 2), ("sum1", 1),
+    ("sum1", 2), ("sum2", 0), ("up", 0), ("sum2", 1), ("sum3", 0), ("grad", 0),
+    ("sum2", 2), ("sum3", 1), ("grad", 1), ("back1", 0), ("sum3", 2), ("send", 1),
+    ("send", 2), ("back1", 1), ("grad", 2), ("back2", 0), ("back1", 2), ("grad", 3),
+    ("grad", 4), ("grad", 5), ("back2", 1), ("grad", 6), ("grad", 7), ("owned", 0),
+    ("back2", 2),
+)
 FAR_FIRST = (10, 6, 9, 11, 14, 5, 7, 13, 15, 2, 8, 1, 3, 4, 12)
 
 
@@ -62,11 +70,11 @@
 
 def kernel(
     n_gx, n_gy, cap,
-    slot_ref, inv_ref, occ_ref, feat, weight, cot,
+    owner_ref, occ_ref, feat, weight, cot,
     ov, gi, ag,
     fp, pt, mk, act, bk, cv, csend, ret, outg, arr, wv, ub, yhu, ysu, uu, upt,
     xs, ys, dwf, s1s, s1r, s2s, s2r, s3s, s3r, pk, pc, po, qs, pysel,
-    sem_feat, sem_in, sem_loc,
+    slot_ref, inv_ref, sem_feat, sem_in, sem_loc,
     a1_s, a1_r, a2_s, a2_r, h_s, h_r, u_s, u_r,
     r1_s, r1_r, r2_s, r2_r, r3_s, r3_r, g4_s, g4_r, g5_s, g5_r, g6_s, g6_r,
 ):
@@ -126,6 +134,63 @@
     _, cbz, cvy, cvz = row_coords(c)
     pysel[...] = as_bf((r < 32) & (cvy == 0) & (4 * cbz + cvz == r))
 
+    def remote(src, dst, s_sem, r_sem, to):
+        return pltpu.make_async_remote_copy(
+            src_ref=src, dst_ref=dst, send_sem=s_sem, recv_sem=r_sem,
+            device_id=to, device_id_type=MESH,
+        )
+
+    def a2a(d, src, dst, s_sem, r_sem):
+        to = peer_j[d]
+        return remote(
+            src.at[pl.ds(to * cap, cap)], dst.at[pl.ds(j * cap, cap)], s_sem.at[d], r_sem.at[d], (i, to)
+        )
+
+    def a2a_arrival(d, src, dst, s_sem, r_sem):
+        frm = peer_j[d]
+        here = pl.ds(frm * cap, cap)
+        return remote(src.at[here], dst.at[here], s_sem.at[d], r_sem.at[d], (i, frm))
+
+    def occ_row(x, y):
+        return occ_ref[x, pl.ds(y, 1), :].astype(F32)
+
+    def lanes_of(rows):
+        return jnp.concatenate(rows, 1)
+
+    def wide(row):
+        return jnp.broadcast_to(row, (16, 256)).astype(BF)
+
+    def masked_rows(mat, row):
+        rows = mat.shape[0]
+        m = wide(row)
+        return (mat.reshape(rows // 16, 16, 256) * m[None]).reshape(rows, 256)
+
+    feat_copy(15).wait()
+    for by in range(2):
+        for py in range(2):
+            row = lanes_of([occ_row(15, 8 * by + 2 * v + py) for v in range(4)])
+            rhs = jnp.concatenate([fp[16, 1 + 8 * by + 2 * v + py] for v in range(4)], 0)
+            res = dot(masked_rows(pc[1], row), rhs).astype(BF)
+            for v in range(4):
+                xs[8 * by + 2 * v + py] = res[64 * v : 64 * v + 64]
+
+    for x in range(14, -1, -1):
+        feat_copy(x).wait()
+
+    def mask_y(x, carry):
+        row = lanes_of([occ_row(x, 9 + 2 * v) for v in range(4)])
+        rhs = jnp.concatenate([fp[x + 1, 10 + 2 * v] for v in range(4)], 0)
+        ys[x] = dot(masked_rows(pc[1, 192:256, :], row), rhs).astype(BF)
+        return carry
+
+    lax.fori_loop(0, 16, mask_y, 0, unroll=4)
+    pl.semaphore_wait(barrier, len(peers))
+    halo_x = remote(xs, fp.at[0, pl.ds(1, 16)], h_s.at[0], h_r.at[0], (nxt_i, j))
+    halo_y = remote(ys, fp.at[pl.ds(1, 16), 0], h_s.at[1], h_r.at[1], (i, nxt_j))
+    halo_c = remote(ys.at[15], fp.at[0, 0], h_s.at[2], h_r.at[2], (nxt_i, nxt_j))
+    halo_y.start()
+    halo_x.start()
+    halo_c.start()
     cot_copy.wait()
 
     def cot_step(n, carry):
@@ -143,63 +208,6 @@
 
     lax.fori_loop(0, 12, cot_step, 0)
 
-    def remote(src, dst, s_sem, r_sem, to):
-        return pltpu.make_async_remote_copy(
-            src_ref=src, dst_ref=dst, send_sem=s_sem, recv_sem=r_sem,
-            device_id=to, device_id_type=MESH,
-        )
-
-    def a2a(d, src, dst, s_sem, r_sem):
-        to = peer_j[d]
-        return remote(
-            src.at[pl.ds(to * cap, cap)], dst.at[pl.ds(j * cap, cap)], s_sem.at[d], r_sem.at[d], (i, to)
-        )
-
-    def a2a_arrival(d, src, dst, s_sem, r_sem):
-        frm = peer_j[d]
-        here = pl.ds(frm * cap, cap)
-        return remote(src.at[here], dst.at[here], s_sem.at[d], r_sem.at[d], (i, frm))
-
-    def occ_row(x, y):
-        return occ_ref[x, pl.ds(y, 1), :].astype(F32)
-
-    def lanes_of(rows):
-        return jnp.concatenate(rows, 1)
-
-    def wide(row):
-        return jnp.broadcast_to(row, (16, 256)).astype(BF)
-
-    def masked_rows(mat, row):
-        rows = mat.shape[0]
-        m = wide(row)
-        return (mat.reshape(rows // 16, 16, 256) * m[None]).reshape(rows, 256)
-
-    feat_copy(15).wait()
-    for by in range(2):
-        for py in range(2):
-            row = lanes_of([occ_row(15, 8 * by + 2 * v + py) for v in range(4)])
-            rhs = jnp.concatenate([fp[16, 1 + 8 * by + 2 * v + py] for v in range(4)], 0)
-            res = dot(masked_rows(pc[1], row), rhs).astype(BF)
-            for v in range(4):
-                xs[8 * by + 2 * v + py] = res[64 * v : 64 * v + 64]
-
-    for x in range(14, -1, -1):
-        feat_copy(x).wait()
-
-    def mask_y(x, carry):
-        row = lanes_of([occ_row(x, 9 + 2 * v) for v in range(4)])
-        rhs = jnp.concatenate([fp[x + 1, 10 + 2 * v] for v in range(4)], 0)
-        ys[x] = dot(masked_rows(pc[1, 192:256, :], row), rhs).astype(BF)
-        return carry
-
-    lax.fori_loop(0, 16, mask_y, 0)
-    pl.semaphore_wait(barrier, len(peers))
-    halo_x = remote(xs, fp.at[0, pl.ds(1, 16)], h_s.at[0], h_r.at[0], (nxt_i, j))
-    halo_y = remote(ys, fp.at[pl.ds(1, 16), 0], h_s.at[1], h_r.at[1], (i, nxt_j))
-    halo_c = remote(ys.at[15], fp.at[0, 0], h_s.at[2], h_r.at[2], (nxt_i, nxt_j))
-    halo_y.start()
-    halo_x.start()
-    halo_c.start()
     for d in order:
         a2a(d, csend, ret, a1_s, a1_r).start()
     own1 = pltpu.make_async_copy(
@@ -271,6 +279,22 @@
 
     lax.fori_loop(0, 8, forward, 0)
 
+    owners = [owner_ref[b] for b in range(32)]
+    for b in range(32):
+        slot = owners[b] * cap
+        for earlier in range(b):
+            slot = slot + jnp.where(owners[earlier] == owners[b], 1, 0)
+        slot_ref[b] = slot
+
+    def invert(s, carry):
+        found = jnp.int32(0)
+        for b in range(32):
+            found = found + jnp.where(slot_ref[b] == s, (b // 16) * 64 + b % 16 + 1, 0)
+        inv_ref[s] = found - 1
+        return carry
+
+    lax.fori_loop(0, n_gy * cap, invert, 0)
+
     def pack(s, carry):
         base = inv_ref[s]
         keep = jnp.where(base >= 0, 1.0, 0.0).astype(F32)
@@ -307,12 +331,14 @@
     up_y.start()
     up_c.start()
 
-    for d in order:
-        a2a(d, outg, arr, a2_s, a2_r).start()
     own2 = pltpu.make_async_copy(
         outg.at[pl.ds(j * cap, cap)], arr.at[pl.ds(j * cap, cap)], sem_loc.at[1]
     )
     own2.start()
+
+    def send(n):
+        for d in order[5 * n : 5 * n + 5]:
+            a2a(d, outg, arr, a2_s, a2_r).start()
 
     for ox in range(8):
         upt[:, ox * 256 : ox * 256 + 256] = dot_nt(pc[1], ub[ox]).astype(BF)
@@ -457,15 +483,6 @@
             stage5_arrival(n, d).wait_recv()
             stage6(n, d).start()
 
-    weight_chunk(0)
-    weight_chunk(1)
-    after1(0)
-    weight_chunk(2)
-    after1(1)
-
-    up_x.wait()
-    up_y.wait()
-    up_c.wait()
     okn_x = jnp.where(i < n_gx - 1, 1.0, 0.0).astype(F32)
     okn_y = jnp.where(j < n_gy - 1, 1.0, 0.0).astype(F32)
 
@@ -480,7 +497,11 @@
         uu[1, ox, :, 256:512] = (dot(qs[2], base) + dot(qs[3, :, 128:256], halo)).astype(BF)
         return carry
 
-    lax.fori_loop(0, 9, shifts, 0)
+    def shift_all(n):
+        up_x.wait()
+        up_y.wait()
+        up_c.wait()
+        lax.fori_loop(0, 9, shifts, 0, unroll=3)
 
     lists = (((1, 0),), ((2, 0), (0, 1)))
 
@@ -512,32 +533,8 @@
                         gi[2 * ox + px, 8 * by + 2 * v + py] = res[64 * v : 64 * v + 64, 128 * by : 128 * by + 128]
         return carry
 
-    def grads(lo, hi):
-        lax.fori_loop(lo, hi, grad_in, 0)
-
-    after1(2)
-    grads(0, 1)
-    after2(0)
-    grads(1, 2)
-    after2(1)
-    after3(0)
-    grads(2, 3)
-    after2(2)
-    after3(1)
-    grads(3, 4)
-    after4(0)
-    after3(2)
-    grads(4, 5)
-    after4(1)
-    grads(5, 6)
-    after5(0)
-    after4(2)
-    grads(6, 8)
-    after5(1)
-
-    own2.wait()
-    for d in order:
-        a2a_arrival(d, outg, arr, a2_s, a2_r).wait_recv()
+    def one_grad(n):
+        grad_in(n, 0)
 
     def owned_step(n, carry):
         t, vg = n // 4, n % 4
@@ -547,9 +544,18 @@
             ov[pl.ds(pl.multiple_of(16 * t, 16), 16), pl.ds(pl.multiple_of(4096 * vg + 256 * v, 256), 256)] = res[16 * v : 16 * v + 16]
         return carry
 
-    lax.fori_loop(0, 12, owned_step, 0)
-
-    after5(2)
+    def owned(n):
+        own2.wait()
+        for d in order:
+            a2a_arrival(d, outg, arr, a2_s, a2_r).wait_recv()
+        lax.fori_loop(0, 12, owned_step, 0, unroll=2)
+
+    steps = dict(
+        weight=weight_chunk, sum1=after1, sum2=after2, sum3=after3, back1=after4, back2=after5,
+        up=shift_all, grad=one_grad, send=send, owned=owned,
+    )
+    for step, n in SCHEDULE:
+        steps[step](n)
     for n in range(len(CHUNKS)):
         for d in range(n_x):
             stage6_arrival(n, d).wait_recv()
@@ -599,13 +605,6 @@
     rows2 = 128 // n_x
     _, tiles, per = chunk_plan(n_x, n_gy)
     slots_n = n_gy * cap
-    targets = owner.reshape(-1)
-    b = jnp.arange(32, dtype=jnp.int32)
-    earlier = (targets[:, None] == targets[None, :]) & (b[:, None] > b[None, :])
-    slots = targets * cap + jnp.sum(earlier.astype(jnp.int32), axis=1)
-    base = (b // 16) * 64 + b % 16
-    hit = jnp.arange(slots_n, dtype=jnp.int32)[:, None] == slots[None, :]
-    inv = jnp.sum(jnp.where(hit, base[None, :] + 1, 0), axis=1) - 1
 
     V = pltpu.VMEM
     D = pltpu.SemaphoreType.DMA
@@ -641,6 +640,8 @@
         V((256, 256), BF),
         V((4, 256, 256), BF),
         V((128, 128), BF),
+        pltpu.SMEM((32,), jnp.int32),
+        pltpu.SMEM((slots_n,), jnp.int32),
         D((16,)), D((2,)), D((2,)),
         D((16,)), D((16,)), D((16,)), D((16,)),
         D((3,)), D((3,)), D((3,)), D((3,)),
@@ -665,7 +666,7 @@
             V((16, 16, 64, 128), BF),
             V((2, n_x, tiles, 16, 128), BF),
         ),
-        in_specs=[smem, smem, vmem, anywhere, anywhere, anywhere],
+        in_specs=[smem, vmem, anywhere, anywhere, anywhere],
         out_specs=[vmem] * 3,
         scratch_shapes=scratch,
         compiler_params=pltpu.CompilerParams(
@@ -674,7 +675,7 @@
         cost_estimate=pl.CostEstimate(
             flops=12_000_000_000, bytes_accessed=20_000_000, transcendentals=0
         ),
-    )(slots, inv, occupancy, features, weight.reshape(TAPS * 128, 256), cotangent)
+    )(owner.reshape(32), occupancy, features, weight.reshape(TAPS * 128, 256), cotangent)
     parts = [pltpu.with_memory_space_constraint(part, pltpu.VMEM) for part in parts]
     owned, gin, gw = pl.pallas_call(
         finish,

time: 98.5 us -> 87.8 us (0.89)
  Pallas kernels: 95.3 us -> 86.8 us
  other arithmetic: 2.18 us -> 0 us
    pallas_call x1, Pallas kernels: 91.3 us -> 82.8 us  [on_device(): pl.pallas_call(body, out_shape=(V((slots_n, 16384), BF), V((16, 16, 64, 1...]
    reduce_sum x2 -> x0, other arithmetic: 1 us -> none  [the longest x1 0.91 us: on_device(): slots = targets * cap + jnp.sum(earlier.astype(jnp.int32), axis=1)]
where the time goes in v2:
time: 87.8 us; the launch traced here: 87.6 us
  Pallas kernels  86.8 us (99%)
    pallas_call x1, Pallas kernels, on_device(): pl.pallas_call(body, out_shape=(V((slots_n, 16384), BF), V((16, 16, 64, 1...  82.8 us
    pallas_call x1, Pallas kernels, on_device(): pl.pallas_call(finish, out_shape=(jax.ShapeDtypeStruct((slots_n, 16384),...  4.02 us

profile of v2, /device:TPU:1, one launch (start us, length us, event | category | flops | bytes accessed | tf_op | source)
XLA Modules:
  0.0 87.6 jit_solution(5139393065282258305)
XLA Ops:
  0.6 82.8 %shard_map.76 = (bf16[48,16384]{1,0:T(8,128)(2,1)S(1)}, bf16[16,16,64,128]{3,2,1,0:T(8,128)(2,1)S(1)}, bf16[2,4,64,16,128]{4,3,2,1,0:T(8,128)(2,1)S(1)}) custom-call(s32[32]{0:T(128)} %bitcast.5, s32[16,16,64]{2,1,0:T(8,128)} %refs_1_.1, bf16[16,16,64,128]{3,2,1,0:T(8,128)(2,1)} %refs_2_.1, bf16[3456,256]{1,0:T(8,128)(2,1)} %bitcast.3, ...), custom_call_target="tpu_custom_call" | custom-call | flops 12000000000 | bytes 20000000 | tf_op jit(solution)/shard_map/pallas_call | solution.py:662
  83.4 4.0 %shard_map.77 = (bf16[48,16384]{1,0:T(8,128)(2,1)}, bf16[16,16,64,128]{3,2,1,0:T(8,128)(2,1)}, f32[27,128,256]{2,1,0:T(8,128)}) custom-call(bf16[48,16384]{1,0:T(8,128)(2,1)S(1)} %get-tuple-element.9.refs_0_, bf16[16,16,64,128]{3,2,1,0:T(8,128)(2,1)S(1)} %get-tuple-element.10.refs_1_, bf16[2,4,64,16,128]{4,3,2,1,0:T(8,128)(2,1)S(1)} %get-tuple-element.11.refs_2_), custom_call_target="tpu_custom_call" | custom-call | flops 500000000 | bytes 10000000 | tf_op jit(solution)/shard_map/pallas_call | solution.py:680

commit v3 on v2

--- a/solution.py
+++ b/solution.py
@@ -15,8 +15,8 @@
     ("sum1", 2), ("sum2", 0), ("up", 0), ("sum2", 1), ("sum3", 0), ("grad", 0),
     ("sum2", 2), ("sum3", 1), ("grad", 1), ("back1", 0), ("sum3", 2), ("send", 1),
     ("send", 2), ("back1", 1), ("grad", 2), ("back2", 0), ("back1", 2), ("grad", 3),
-    ("grad", 4), ("grad", 5), ("back2", 1), ("grad", 6), ("grad", 7), ("owned", 0),
-    ("back2", 2),
+    ("grad", 4), ("grad", 5), ("back2", 1), ("grad", 6), ("grad", 7), ("back2", 2),
+    ("owned", 0),
 )
 FAR_FIRST = (10, 6, 9, 11, 14, 5, 7, 13, 15, 2, 8, 1, 3, 4, 12)
 

time: 87.8 us -> 86.2 us (0.982)
  Pallas kernels: 86.8 us -> 85.3 us
    pallas_call x1, Pallas kernels: 82.8 us -> 81.3 us  [on_device(): pl.pallas_call(body, out_shape=(V((slots_n, 16384), BF), V((16, 16, 64, 1...]
where the time goes in v3:
time: 86.2 us; the launch traced here: 86.1 us
  Pallas kernels  85.3 us (99%)
    pallas_call x1, Pallas kernels, on_device(): pl.pallas_call(body, out_shape=(V((slots_n, 16384), BF), V((16, 16, 64, 1...  81.3 us
    pallas_call x1, Pallas kernels, on_device(): pl.pallas_call(finish, out_shape=(jax.ShapeDtypeStruct((slots_n, 16384),...  4.02 us

profile of v3, /device:TPU:1, one launch (start us, length us, event | category | flops | bytes accessed | tf_op | source)
XLA Modules:
  0.0 86.1 jit_solution(1432574543854170249)
XLA Ops:
  0.6 81.3 %shard_map.76 = (bf16[48,16384]{1,0:T(8,128)(2,1)S(1)}, bf16[16,16,64,128]{3,2,1,0:T(8,128)(2,1)S(1)}, bf16[2,4,64,16,128]{4,3,2,1,0:T(8,128)(2,1)S(1)}) custom-call(s32[32]{0:T(128)} %bitcast.5, s32[16,16,64]{2,1,0:T(8,128)} %refs_1_.1, bf16[16,16,64,128]{3,2,1,0:T(8,128)(2,1)} %refs_2_.1, bf16[3456,256]{1,0:T(8,128)(2,1)} %bitcast.3, ...), custom_call_target="tpu_custom_call" | custom-call | flops 12000000000 | bytes 20000000 | tf_op jit(solution)/shard_map/pallas_call | solution.py:662
  81.9 4.0 %shard_map.77 = (bf16[48,16384]{1,0:T(8,128)(2,1)}, bf16[16,16,64,128]{3,2,1,0:T(8,128)(2,1)}, f32[27,128,256]{2,1,0:T(8,128)}) custom-call(bf16[48,16384]{1,0:T(8,128)(2,1)S(1)} %get-tuple-element.9.refs_0_, bf16[16,16,64,128]{3,2,1,0:T(8,128)(2,1)S(1)} %get-tuple-element.10.refs_1_, bf16[2,4,64,16,128]{4,3,2,1,0:T(8,128)(2,1)S(1)} %get-tuple-element.11.refs_2_), custom_call_target="tpu_custom_call" | custom-call | flops 500000000 | bytes 10000000 | tf_op jit(solution)/shard_map/pallas_call | solution.py:680

commit v4 on v3

--- a/solution.py
+++ b/solution.py
@@ -12,10 +12,10 @@
 CHUNKS = ((0, 8), (8, 16), (16, 27))
 SCHEDULE = (
     ("send", 0), ("weight", 0), ("weight", 1), ("sum1", 0), ("weight", 2), ("sum1", 1),
-    ("sum1", 2), ("sum2", 0), ("up", 0), ("sum2", 1), ("sum3", 0), ("grad", 0),
-    ("sum2", 2), ("sum3", 1), ("grad", 1), ("back1", 0), ("sum3", 2), ("send", 1),
-    ("send", 2), ("back1", 1), ("grad", 2), ("back2", 0), ("back1", 2), ("grad", 3),
-    ("grad", 4), ("grad", 5), ("back2", 1), ("grad", 6), ("grad", 7), ("back2", 2),
+    ("sum1", 2), ("sum2", 0), ("up", 0), ("grad", 0), ("sum2", 1), ("sum3", 0),
+    ("grad", 1), ("sum2", 2), ("sum3", 1), ("grad", 2), ("back1", 0), ("sum3", 2),
+    ("send", 1), ("send", 2), ("back1", 1), ("grad", 3), ("grad", 4), ("back2", 0),
+    ("back1", 2), ("grad", 5), ("grad", 6), ("back2", 1), ("grad", 7), ("back2", 2),
     ("owned", 0),
 )
 FAR_FIRST = (10, 6, 9, 11, 14, 5, 7, 13, 15, 2, 8, 1, 3, 4, 12)
@@ -337,7 +337,7 @@
     own2.start()
 
     def send(n):
-        for d in order[5 * n : 5 * n + 5]:
+        for d in order[(0, 4, 9)[n] : (4, 9, 15)[n]]:
             a2a(d, outg, arr, a2_s, a2_r).start()
 
     for ox in range(8):

time: 86.2 us -> 88.9 us (1.031)
  Pallas kernels: 85.3 us -> 87.9 us
    pallas_call x1, Pallas kernels: 81.3 us -> 83.9 us  [on_device(): pl.pallas_call(body, out_shape=(V((slots_n, 16384), BF), V((16, 16, 64, 1...]
where the time goes in v4:
time: 88.9 us; the launch traced here: 88.7 us
  Pallas kernels  87.9 us (99%)
    pallas_call x1, Pallas kernels, on_device(): pl.pallas_call(body, out_shape=(V((slots_n, 16384), BF), V((16, 16, 64, 1...  83.9 us
    pallas_call x1, Pallas kernels, on_device(): pl.pallas_call(finish, out_shape=(jax.ShapeDtypeStruct((slots_n, 16384),...  4.01 us

profile of v4, /device:TPU:1, one launch (start us, length us, event | category | flops | bytes accessed | tf_op | source)
XLA Modules:
  0.0 88.7 jit_solution(5877428162790932971)
XLA Ops:
  0.6 83.9 %shard_map.76 = (bf16[48,16384]{1,0:T(8,128)(2,1)S(1)}, bf16[16,16,64,128]{3,2,1,0:T(8,128)(2,1)S(1)}, bf16[2,4,64,16,128]{4,3,2,1,0:T(8,128)(2,1)S(1)}) custom-call(s32[32]{0:T(128)} %bitcast.5, s32[16,16,64]{2,1,0:T(8,128)} %refs_1_.1, bf16[16,16,64,128]{3,2,1,0:T(8,128)(2,1)} %refs_2_.1, bf16[3456,256]{1,0:T(8,128)(2,1)} %bitcast.3, ...), custom_call_target="tpu_custom_call" | custom-call | flops 12000000000 | bytes 20000000 | tf_op jit(solution)/shard_map/pallas_call | solution.py:662
  84.5 4.0 %shard_map.77 = (bf16[48,16384]{1,0:T(8,128)(2,1)}, bf16[16,16,64,128]{3,2,1,0:T(8,128)(2,1)}, f32[27,128,256]{2,1,0:T(8,128)}) custom-call(bf16[48,16384]{1,0:T(8,128)(2,1)S(1)} %get-tuple-element.9.refs_0_, bf16[16,16,64,128]{3,2,1,0:T(8,128)(2,1)S(1)} %get-tuple-element.10.refs_1_, bf16[2,4,64,16,128]{4,3,2,1,0:T(8,128)(2,1)S(1)} %get-tuple-element.11.refs_2_), custom_call_target="tpu_custom_call" | custom-call | flops 500000000 | bytes 10000000 | tf_op jit(solution)/shard_map/pallas_call | solution.py:680
